TPU v7x, 32 devices: a whole 2x2x4 slice. The times are simulated.
32 devices in a mesh: dp: 8 (over y, x, core), tensor: 4 (over z).
Axes of the slice: x: 2, y: 2, z: 4, core: 2. Of those that a mesh axis runs over, the one named last changes fastest.
Arguments:
- tokens: bfloat16 [1024, 8, 1024], P('tensor', 'dp'), may hold values from -6 to 6
- cotangent: bfloat16 [1024, 8, 1024], P('tensor', 'dp'), may hold values from -6 to 6
- clip_mask: int32 [8], P('dp'), may hold values from 0 to 1, as said below
- positions: int32 [3, 8, 1024], P(None, 'dp'), may hold values from 0 to 15
- triple_weight: bfloat16 [2, 1024, 3, 1024], P(None, 'dp', None, 'tensor'), may hold values from -0.1875 to 0.1875
- triple_bias: bfloat16 [2, 3, 1024], P(None, None, 'tensor'), may hold values from -0.75 to 0.75
- exit_weight: bfloat16 [2, 1024, 1024], P(None, 'tensor', 'dp'), may hold values from -2 to 2
- expand_weight: bfloat16 [2, 1024, 4096], P(None, 'dp', 'tensor'), may hold values from -0.1875 to 0.1875
- expand_bias: bfloat16 [2, 4096], P(None, 'tensor'), may hold values from -4 to 4
- shrink_weight: bfloat16 [2, 4096, 1024], P(None, 'tensor', 'dp'), may hold values from -0.09375 to 0.09375
- norm_gain: bfloat16 [2, 2, 1024], replicated, may hold values from 0.5 to 1.5
- norm_shift: bfloat16 [2, 2, 1024], replicated, may hold values from -3 to 3
- branch_bias: bfloat16 [2, 2, 1024], replicated, may hold values from -4 to 4
Outputs:
- mixed: float32 [1024, 8, 1024], P('tensor', 'dp')
- tokens_gradient: float32 [1024, 8, 1024], P('tensor', 'dp')
- triple_gradient: float32 [2, 1024, 3, 1024], P(None, 'dp', None, 'tensor')
- triple_bias_gradient: float32 [2, 3, 1024], P(None, None, 'tensor')
- exit_gradient: float32 [2, 1024, 1024], P(None, 'tensor', 'dp')
- expand_gradient: float32 [2, 1024, 4096], P(None, 'dp', 'tensor')
- expand_bias_gradient: float32 [2, 4096], P(None, 'tensor')
- shrink_gradient: float32 [2, 4096, 1024], P(None, 'tensor', 'dp')
- gain_gradient: float32 [2, 2, 1024], replicated
- shift_gradient: float32 [2, 2, 1024], replicated
- branch_bias_gradient: float32 [2, 2, 1024], replicated
Inputs may be any that keep to these rules, and one draw needn't show every extreme that they name: `clip_mask`: exactly 1 of the 8 slots hold 0.
All inputs are finite; a program needn't handle non-finite values.
Results may differ from a plain program's by a relative error of at most 0.015.
Values may be sent and summed in bfloat16 or wider, within the bound.
A program may use at most 128 MiB of HBM per device.

v0:
```python
import jax
import jax.numpy as jnp
from jax import lax
from jax.sharding import PartitionSpec as P

HEAD_DIM = 64
ROT = 20
LAYERS = 2
SEQ = 1024
QBLOCK = 512
EPSILON = 1e-06
SQRT_HALF = 0.7071067811865476
ROOT_TWO_PI = 2.5066282746310002


def rotary_tables(positions):
    halfway = ROT // 2
    indices = jnp.arange(halfway, dtype=jnp.float32)
    frequency = 10000.0 ** (-indices / halfway)
    angles = jnp.transpose(positions.astype(jnp.float32), (0, 2, 1))[..., None] * frequency
    return (jnp.cos(angles)[:, :, :, None, :], jnp.sin(angles)[:, :, :, None, :])


def rotate(values, cosines, sines):
    halfway = ROT // 2
    pieces = []
    for coord_index in range(3):
        offset = coord_index * ROT
        former = values[..., offset : offset + halfway]
        latter = values[..., offset + halfway : offset + ROT]
        pieces.append(former * cosines[coord_index] - latter * sines[coord_index])
        pieces.append(latter * cosines[coord_index] + former * sines[coord_index])
    pieces.append(values[..., 3 * ROT :])
    return jnp.concatenate(pieces, axis=-1)


def normalize(values, gain_row, shift_row):
    center = values - jnp.mean(values, axis=-1, keepdims=True)
    inverse = lax.rsqrt(jnp.mean(center * center, axis=-1, keepdims=True) + EPSILON)
    scaled = center * inverse
    return (scaled * gain_row + shift_row, scaled, inverse)


def norm_back(upstream, scaled, inverse, gain_row):
    weighted = upstream * gain_row
    first_mean = jnp.mean(weighted, axis=-1, keepdims=True)
    second_mean = jnp.mean(weighted * scaled, axis=-1, keepdims=True)
    return inverse * (weighted - first_mean - scaled * second_mean)


def gelu_slope(inner_sum):
    return (
        0.5 * (1.0 + lax.erf(inner_sum * SQRT_HALF))
        + inner_sum * jnp.exp(-0.5 * inner_sum * inner_sum) / ROOT_TWO_PI
    )


def to_items(array):
    seq_length, clip_count, head_count, head_width = array.shape
    return jnp.transpose(array, (1, 2, 0, 3)).reshape(
        clip_count * head_count, seq_length, head_width
    )


def from_items(array, clip_count):
    item_count, seq_length, head_width = array.shape
    return jnp.transpose(
        array.reshape(clip_count, item_count // clip_count, seq_length, head_width), (2, 0, 1, 3)
    )


def attend(queries, key_items, values):
    factor = HEAD_DIM ** (-0.5)
    block_count = SEQ // QBLOCK

    def one_item(triple):
        query_rows, key_rows, value_rows = triple

        def one_block(query_block):
            scores = (
                jnp.einsum("qe,ke->qk", query_block, key_rows, preferred_element_type=jnp.float32)
                * factor
            )
            highest = jnp.max(scores, axis=-1, keepdims=True)
            weights = jnp.exp(scores - highest)
            summed = jnp.sum(weights, axis=-1, keepdims=True)
            chances = (weights / summed).astype(jnp.bfloat16)
            output = jnp.einsum(
                "qk,ke->qe", chances, value_rows, preferred_element_type=jnp.float32
            )
            return (output.astype(jnp.bfloat16), (highest + jnp.log(summed))[:, 0])

        outputs, logsums = lax.map(one_block, query_rows.reshape(block_count, QBLOCK, HEAD_DIM))
        return (outputs.reshape(SEQ, HEAD_DIM), logsums.reshape(SEQ))

    return lax.map(one_item, (queries, key_items, values))


def attend_back(queries, key_items, values, out_grads, logsums):
    factor = HEAD_DIM ** (-0.5)
    block_count = SEQ // QBLOCK

    def one_item(group):
        query_rows, key_rows, value_rows, grad_rows, logsum_rows = group

        def one_block(carry, blocked):
            key_total, value_total = carry
            query_block, grad_block, logsum_block = blocked
            scores = (
                jnp.einsum("qe,ke->qk", query_block, key_rows, preferred_element_type=jnp.float32)
                * factor
            )
            chances = jnp.exp(scores - logsum_block[:, None])
            value_total = value_total + jnp.einsum(
                "qk,qe->ke",
                chances.astype(jnp.bfloat16),
                grad_block,
                preferred_element_type=jnp.float32,
            )
            chance_grad = jnp.einsum(
                "qe,ke->qk", grad_block, value_rows, preferred_element_type=jnp.float32
            )
            center = jnp.sum(chances * chance_grad, axis=-1, keepdims=True)
            score_grad = (chances * (chance_grad - center)).astype(jnp.bfloat16)
            query_grad = (
                jnp.einsum("qk,ke->qe", score_grad, key_rows, preferred_element_type=jnp.float32)
                * factor
            )
            key_total = (
                key_total
                + jnp.einsum(
                    "qk,qe->ke", score_grad, query_block, preferred_element_type=jnp.float32
                )
                * factor
            )
            return ((key_total, value_total), query_grad)

        zeros = jnp.zeros((SEQ, HEAD_DIM), jnp.float32)
        blocked_rows = (
            query_rows.reshape(block_count, QBLOCK, HEAD_DIM),
            grad_rows.reshape(block_count, QBLOCK, HEAD_DIM),
            logsum_rows.reshape(block_count, QBLOCK),
        )
        (key_total, value_total), query_grads = lax.scan(one_block, (zeros, zeros), blocked_rows)
        return (query_grads.reshape(SEQ, HEAD_DIM), key_total, value_total)

    return lax.map(one_item, (queries, key_items, values, out_grads, logsums))


def shards(
    tokens,
    cotangent,
    clip_mask,
    positions,
    triple_weight,
    triple_bias,
    exit_weight,
    expand_weight,
    expand_bias,
    shrink_weight,
    norm_gain,
    norm_shift,
    branch_bias,
):
    row_count = tokens.shape[0]
    clip_count = tokens.shape[1]
    local_width = triple_weight.shape[3]
    head_count = local_width // HEAD_DIM
    cosines, sines = rotary_tables(positions)
    live = clip_mask.astype(jnp.float32)[None, :, None]

    def spread_rows(normed):
        return lax.all_gather(normed, "tensor", axis=0, tiled=True)

    def spread_grads(upstream_low):
        return lax.all_gather(upstream_low, "tensor", axis=0, tiled=True)

    def collect_rows(operand, matrix, pattern):

        def partial_term(offset, row_span):
            return jnp.einsum(pattern, operand, matrix, preferred_element_type=jnp.float32)

        return lax.psum_scatter(
            partial_term(jnp.int32(0), row_count * lax.axis_size("tensor")).astype(jnp.bfloat16),
            "tensor",
            scatter_dimension=0,
            tiled=True,
        ).astype(jnp.float32)

    def collect_grads(operand, matrix, pattern):

        def partial_term(offset, row_span):
            return jnp.einsum(pattern, operand, matrix, preferred_element_type=jnp.float32)

        return lax.psum_scatter(
            partial_term(jnp.int32(0), row_count * lax.axis_size("tensor")).astype(jnp.bfloat16),
            "tensor",
            scatter_dimension=0,
            tiled=True,
        ).astype(jnp.float32)

    hidden = tokens.astype(jnp.float32)
    saved = []
    for layer_index in range(LAYERS):
        fetched = (
            lax.all_gather(triple_weight[layer_index], "dp", axis=0, tiled=True),
            lax.all_gather(exit_weight[layer_index], "dp", axis=1, tiled=True),
            lax.all_gather(expand_weight[layer_index], "dp", axis=0, tiled=True),
            lax.all_gather(shrink_weight[layer_index], "dp", axis=1, tiled=True),
        )
        triple_full, exit_full, expand_full, shrink_full = fetched
        gain_pair = norm_gain[layer_index].astype(jnp.float32)
        shift_pair = norm_shift[layer_index].astype(jnp.float32)
        bias_pair = branch_bias[layer_index].astype(jnp.float32)
        normed, scaled_one, inverse_one = normalize(hidden, gain_pair[0], shift_pair[0])
        gathered_one = spread_rows(normed.astype(jnp.bfloat16))
        mixed_triple = jnp.einsum(
            "scd,dtf->sctf", gathered_one, triple_full, preferred_element_type=jnp.float32
        ) + triple_bias[layer_index].astype(jnp.float32)
        split_heads = mixed_triple.reshape(SEQ, clip_count, 3, head_count, HEAD_DIM)
        query_items = to_items(rotate(split_heads[:, :, 0], cosines, sines).astype(jnp.bfloat16))
        key_items = to_items(rotate(split_heads[:, :, 1], cosines, sines).astype(jnp.bfloat16))
        value_items = to_items(split_heads[:, :, 2].astype(jnp.bfloat16))
        attended_items, logsums = attend(query_items, key_items, value_items)
        attended = from_items(attended_items, clip_count).reshape(SEQ, clip_count, local_width)
        hidden = hidden + (collect_rows(attended, exit_full, "sce,ed->scd") + bias_pair[0])
        normed, scaled_two, inverse_two = normalize(hidden, gain_pair[1], shift_pair[1])
        gathered_two = spread_rows(normed.astype(jnp.bfloat16))
        inner_sum = jnp.einsum(
            "scd,df->scf", gathered_two, expand_full, preferred_element_type=jnp.float32
        ) + expand_bias[layer_index].astype(jnp.float32)
        activated = jax.nn.gelu(inner_sum, approximate=False).astype(jnp.bfloat16)
        hidden = hidden + (collect_rows(activated, shrink_full, "scf,fd->scd") + bias_pair[1])
        saved.append(
            (
                gathered_one,
                scaled_one,
                inverse_one,
                query_items,
                key_items,
                value_items,
                logsums,
                attended,
                scaled_two,
                inverse_two,
                gathered_two,
                inner_sum,
                activated,
                fetched,
            )
        )
    mixed = hidden * live
    upstream = cotangent.astype(jnp.float32) * live
    collected = [None] * LAYERS
    gain_parts = [None] * LAYERS
    shift_parts = [None] * LAYERS
    bias_parts = [None] * LAYERS
    triple_bias_parts = [None] * LAYERS
    expand_bias_parts = [None] * LAYERS
    for layer_index in reversed(range(LAYERS)):
        (
            gathered_one,
            scaled_one,
            inverse_one,
            query_items,
            key_items,
            value_items,
            logsums,
            attended,
            scaled_two,
            inverse_two,
            gathered_two,
            inner_sum,
            activated,
            fetched,
        ) = saved[layer_index]
        triple_full, exit_full, expand_full, shrink_full = (
            lax.all_gather(triple_weight[layer_index], "dp", axis=0, tiled=True),
            lax.all_gather(exit_weight[layer_index], "dp", axis=1, tiled=True),
            lax.all_gather(expand_weight[layer_index], "dp", axis=0, tiled=True),
            lax.all_gather(shrink_weight[layer_index], "dp", axis=1, tiled=True),
        )
        gain_pair = norm_gain[layer_index].astype(jnp.float32)
        shrink_low = upstream.astype(jnp.bfloat16)
        bias_two = jnp.sum(shrink_low, axis=(0, 1), dtype=jnp.float32)
        full_grad = spread_grads(shrink_low)
        shrink_grad = jnp.einsum(
            "scf,scd->fd", activated, full_grad, preferred_element_type=jnp.float32
        )
        active_grad = jnp.einsum(
            "scd,fd->scf", full_grad, shrink_full, preferred_element_type=jnp.float32
        )
        inner_low = (active_grad * gelu_slope(inner_sum)).astype(jnp.bfloat16)
        expand_bias_parts[layer_index] = jnp.sum(inner_low, axis=(0, 1), dtype=jnp.float32)
        expand_grad = jnp.einsum(
            "scd,scf->df", gathered_two, inner_low, preferred_element_type=jnp.float32
        )
        normed_grad = collect_grads(inner_low, expand_full, "scf,df->scd")
        gain_two = jnp.sum(normed_grad * scaled_two, axis=(0, 1))
        shift_two = jnp.sum(normed_grad, axis=(0, 1))
        upstream = upstream + norm_back(normed_grad, scaled_two, inverse_two, gain_pair[1])
        branch_low = upstream.astype(jnp.bfloat16)
        bias_one = jnp.sum(branch_low, axis=(0, 1), dtype=jnp.float32)
        full_grad = spread_grads(branch_low)
        exit_grad = jnp.einsum(
            "sce,scd->ed", attended, full_grad, preferred_element_type=jnp.float32
        )
        attended_grad = jnp.einsum(
            "scd,ed->sce", full_grad, exit_full, preferred_element_type=jnp.float32
        ).astype(jnp.bfloat16)
        grad_items = to_items(attended_grad.reshape(SEQ, clip_count, head_count, HEAD_DIM))
        query_grad, key_grad, value_grad = attend_back(
            query_items, key_items, value_items, grad_items, logsums
        )
        query_back = rotate(from_items(query_grad, clip_count), cosines, -sines)
        key_back = rotate(from_items(key_grad, clip_count), cosines, -sines)
        value_back = from_items(value_grad, clip_count)
        triple_low = (
            jnp.stack([query_back, key_back, value_back], axis=2)
            .reshape(SEQ, clip_count, 3, local_width)
            .astype(jnp.bfloat16)
        )
        triple_bias_parts[layer_index] = jnp.sum(triple_low, axis=(0, 1), dtype=jnp.float32)
        triple_grad = jnp.einsum(
            "scd,sctf->dtf", gathered_one, triple_low, preferred_element_type=jnp.float32
        )
        normed_grad = collect_grads(triple_low, triple_full, "sctf,dtf->scd")
        gain_one = jnp.sum(normed_grad * scaled_one, axis=(0, 1))
        shift_one = jnp.sum(normed_grad, axis=(0, 1))
        upstream = upstream + norm_back(normed_grad, scaled_one, inverse_one, gain_pair[0])
        gain_parts[layer_index] = jnp.stack([gain_one, gain_two])
        shift_parts[layer_index] = jnp.stack([shift_one, shift_two])
        bias_parts[layer_index] = jnp.stack([bias_one, bias_two])
        collected[layer_index] = (
            lax.psum_scatter(triple_grad, "dp", scatter_dimension=0, tiled=True),
            lax.psum_scatter(exit_grad, "dp", scatter_dimension=1, tiled=True),
            lax.psum_scatter(expand_grad, "dp", scatter_dimension=0, tiled=True),
            lax.psum_scatter(shrink_grad, "dp", scatter_dimension=1, tiled=True),
        )
    stacked = [
        jnp.stack([collected[layer_index][member] for layer_index in range(LAYERS)])
        for member in range(4)
    ]
    triple_total, exit_total, expand_total, shrink_total = stacked
    gain_total, shift_total, bias_total = lax.psum(
        (jnp.stack(gain_parts), jnp.stack(shift_parts), jnp.stack(bias_parts)), ("dp", "tensor")
    )
    triple_bias_total, expand_bias_total = lax.psum(
        (jnp.stack(triple_bias_parts), jnp.stack(expand_bias_parts)), "dp"
    )
    return (
        mixed,
        upstream,
        triple_total,
        triple_bias_total,
        exit_total,
        expand_total,
        expand_bias_total,
        shrink_total,
        gain_total,
        shift_total,
        bias_total,
    )


def solution(mesh):
    return jax.shard_map(
        shards,
        mesh=mesh,
        in_specs=(
            P("tensor", "dp", None),
            P("tensor", "dp", None),
            P("dp"),
            P(None, "dp", None),
            P(None, "dp", None, "tensor"),
            P(None, None, "tensor"),
            P(None, "tensor", "dp"),
            P(None, "dp", "tensor"),
            P(None, "tensor"),
            P(None, "tensor", "dp"),
            P(),
            P(),
            P(),
        ),
        out_specs=(
            P("tensor", "dp", None),
            P("tensor", "dp", None),
            P(None, "dp", None, "tensor"),
            P(None, None, "tensor"),
            P(None, "tensor", "dp"),
            P(None, "dp", "tensor"),
            P(None, "tensor"),
            P(None, "tensor", "dp"),
            P(),
            P(),
            P(),
        ),
        check_vma=False,
    )
```

profile of v0, /device:TPU:0, one launch (start us, length us, event | category | flops | bytes accessed | tf_op | source)
XLA Modules:
  0.0 1529.0 jit_solution(13057020448451312139)
XLA Ops:
  18.6 13.0 all-gather.1
  32.4 7.3 all-gather.39.cloned.1.call-done
  39.7 48.1 %all-gather.23.cloned.1.call-done = bf16[1024,1,1024]{2,0,1:T(8,128)(2,1)} async-done(((bf16[256,1,1024]{2,0,1:T(8,128)(2,1)}), bf16[1024,1,1024]{2,0,1:T(8,128)(2,1)}) %all-gather.23.cloned.1.call-update) | async-done | bytes 2097168 | tf_op jit(solution)/shard_map/all_gather | solution.py:173
  94.5 12.1 concatenate.87
  110.9 28.1 %while.107 = (s32[]{:T(128)}, bf16[4,1024,64]{1,2,0:T(8,128)(2,1)}, f32[4,1024]{1,0:T(4,128)}, bf16[4,1024,64]{2,1,0:T(8,128)(2,1)S(1)}, bf16[4,1024,64]{2,1,0:T...) while((s32[]{:T(128)}, bf16[4,1024,64]{1,2,0:T(8,128)(2,1)}, ...), condition=%wide.region_7.8_spmd, body=%wide.region_2.7_spmd.sunk | while | flops 138968576 | bytes 8622382 | solution.py:96
  145.6 40.1 %reduce-scatter.17.cloned.1.call-done = bf16[256,1,1024]{2,0,1:T(8,128)(2,1)} async-done(((bf16[1024,1,1024]{2,0,1:T(8,128)(2,1)}), bf16[256,1,1024]{2,0,1:T(8,128)(2,1)}) %reduce-scatter.17.cloned.1.call-update) | async-done | bytes 524304 | tf_op jit(solution)/shard_map/reduce_scatter | solution.py:183
  193.5 22.0 %all-gather.41.cloned.1.call-done = bf16[1,1024,1024]{2,1,0:T(8,128)(2,1)} async-done(((bf16[1,128,1024]{2,1,0:T(8,128)(2,1)}), bf16[1,1024,1024]{2,1,0:T(8,128)(2,1)}) %all-gather.41.cloned.1.call-update) | async-done | bytes 2097168 | tf_op jit(solution)/shard_map/all_gather | solution.py:208
  215.5 48.0 %all-gather.25.cloned.1.call-done = bf16[1024,1,1024]{2,0,1:T(8,128)(2,1)} async-done(((bf16[256,1,1024]{2,0,1:T(8,128)(2,1)}), bf16[1024,1,1024]{2,0,1:T(8,128)(2,1)}) %all-gather.25.cloned.1.call-update) | async-done | bytes 2097168 | tf_op jit(solution)/shard_map/all_gather | solution.py:173
  263.5 14.5 fusion.52
  278.0 14.9 all-gather.43.cloned.1.call-done
  292.9 6.0 convert_bitcast_fusion.4
  299.9 43.1 %reduce-scatter.19.cloned.1.call-done = bf16[256,1,1024]{2,0,1:T(8,128)(2,1)} async-done(((bf16[1024,1,1024]{2,0,1:T(8,128)(2,1)}), bf16[256,1,1024]{2,0,1:T(8,128)(2,1)}) %reduce-scatter.19.cloned.1.call-update) | async-done | bytes 524304 | tf_op jit(solution)/shard_map/reduce_scatter | solution.py:183
  345.8 12.7 all-gather.5
  358.5 12.1 all-gather.45.cloned.1.call-done
  370.6 48.1 %all-gather.27.cloned.1.call-done = bf16[1024,1,1024]{2,0,1:T(8,128)(2,1)} async-done(((bf16[256,1,1024]{2,0,1:T(8,128)(2,1)}), bf16[1024,1,1024]{2,0,1:T(8,128)(2,1)}) %all-gather.27.cloned.1.call-update) | async-done | bytes 2097168 | tf_op jit(solution)/shard_map/all_gather | solution.py:173
  426.2 7.8 concatenate.89
  437.2 26.0 %while.109 = (s32[]{:T(128)}, bf16[4,1024,64]{1,2,0:T(8,128)(2,1)S(1)}, f32[4,1024]{1,0:T(4,128)}, bf16[4,1024,64]{2,1,0:T(8,128)(2,1)S(1)}, bf16[4,1024,64]{2,1...) while((s32[]{:T(128)}, ...), condition=%wide.region_19.20_spmd, body=%wide.region_14.19_spmd.sunk | while | flops 138968576 | bytes 8622382 | solution.py:96
  467.6 42.0 %reduce-scatter.21.cloned.1.call-done = bf16[256,1,1024]{2,0,1:T(8,128)(2,1)} async-done(((bf16[1024,1,1024]{2,0,1:T(8,128)(2,1)}), bf16[256,1,1024]{2,0,1:T(8,128)(2,1)}) %reduce-scatter.21.cloned.1.call-update) | async-done | bytes 524304 | tf_op jit(solution)/shard_map/reduce_scatter | solution.py:183
  515.2 24.2 %all-gather.47.cloned.1.call-done = bf16[1,1024,1024]{2,1,0:T(8,128)(2,1)} async-done(((bf16[1,128,1024]{2,1,0:T(8,128)(2,1)}), bf16[1,1024,1024]{2,1,0:T(8,128)(2,1)}) %all-gather.47.cloned.1.call-update) | async-done | bytes 2097168 | tf_op jit(solution)/shard_map/all_gather | solution.py:208
  539.4 48.0 %all-gather.29.cloned.1.call-done = bf16[1024,1,1024]{2,0,1:T(8,128)(2,1)} async-done(((bf16[256,1,1024]{2,0,1:T(8,128)(2,1)}), bf16[1024,1,1024]{2,0,1:T(8,128)(2,1)}) %all-gather.29.cloned.1.call-update) | async-done | bytes 2097168 | tf_op jit(solution)/shard_map/all_gather | solution.py:173
  587.4 14.5 fusion.55
  602.0 31.7 %all-gather.31.cloned.1.call-done = bf16[1024,1,1024]{2,0,1:T(8,128)(2,1)} async-done(((bf16[256,1,1024]{2,0,1:T(8,128)(2,1)}), bf16[1024,1,1024]{2,0,1:T(8,128)(2,1)}) %all-gather.31.cloned.1.call-update) | async-done | bytes 2097168 | tf_op jit(solution)/shard_map/all_gather | solution.py:176
  633.7 28.9 %all-gather.49.cloned.1.call-done = bf16[1,1024,1024]{2,1,0:T(8,128)(2,1)} async-done(((bf16[1,1024,128]{2,1,0:T(8,128)(2,1)}), bf16[1,1024,1024]{2,1,0:T(8,128)(2,1)}) %all-gather.49.cloned.1.call-update) | async-done | bytes 2097168 | tf_op jit(solution)/shard_map/all_gather | solution.py:209
  662.6 7.2 convert_reduce_fusion
  674.9 5.9 convert_bitcast_fusion.2
  680.9 38.0 %reduce-scatter.25.cloned.1.call-done = bf16[256,1,1024]{2,0,1:T(8,128)(2,1)} async-done(((bf16[1024,1,1024]{2,0,1:T(8,128)(2,1)}), bf16[256,1,1024]{2,0,1:T(8,128)(2,1)}) %reduce-scatter.25.cloned.1.call-update) | async-done | bytes 524304 | tf_op jit(solution)/shard_map/reduce_scatter | solution.py:195
  721.0 43.2 %reduce-scatter.23.cloned.1.call-done = bf16[256,1,1024]{2,0,1:T(8,128)(2,1)} async-done(((bf16[1024,1,1024]{2,0,1:T(8,128)(2,1)}), bf16[256,1,1024]{2,0,1:T(8,128)(2,1)}) %reduce-scatter.23.cloned.1.call-update) | async-done | bytes 524304 | tf_op jit(solution)/shard_map/reduce_scatter | solution.py:183
  770.0 43.6 %all-gather.33.cloned.1.call-done = bf16[1024,1,1024]{2,0,1:T(8,128)(2,1)} async-done(((bf16[256,1,1024]{2,0,1:T(8,128)(2,1)}), bf16[1024,1,1024]{2,0,1:T(8,128)(2,1)}) %all-gather.33.cloned.1.call-update) | async-done | bytes 2097168 | tf_op jit(solution)/shard_map/all_gather | solution.py:176
  818.6 45.1 %while.111 = (s32[]{:T(128)}, f32[4,1024,64]{1,2,0:T(8,128)}, f32[4,1024,64]{1,2,0:T(8,128)S(1)}, bf16[4,1024,64]{1,2,0:T(8,128)(2,1)S(1)}, bf16[4,1024,64]{2,1,...) while((s32[]{:T(128)}, f32[4,1024,64]{1,2,0:T(8,128)}, ...), condition=%wide.region_31.32_spmd, body=%wide.region_27.31_spmd.sunk | while | flops 340098560 | bytes 21916056 | solution.py:147
  878.1 42.7 %reduce-scatter.27.cloned.1.call-done = bf16[256,1,1024]{2,0,1:T(8,128)(2,1)} async-done(((bf16[1024,1,1024]{2,0,1:T(8,128)(2,1)}), bf16[256,1,1024]{2,0,1:T(8,128)(2,1)}) %reduce-scatter.27.cloned.1.call-update) | async-done | bytes 524304 | tf_op jit(solution)/shard_map/reduce_scatter | solution.py:195
  926.3 45.0 %all-gather.35.cloned.1.call-done = bf16[1024,1,1024]{2,0,1:T(8,128)(2,1)} async-done(((bf16[256,1,1024]{2,0,1:T(8,128)(2,1)}), bf16[1024,1,1024]{2,0,1:T(8,128)(2,1)}) %all-gather.35.cloned.1.call-update) | async-done | bytes 2097168 | tf_op jit(solution)/shard_map/all_gather | solution.py:176
  971.3 7.2 convert_reduce_fusion.1
  983.7 42.7 %reduce-scatter.29.cloned.1.call-done = bf16[256,1,1024]{2,0,1:T(8,128)(2,1)} async-done(((bf16[1024,1,1024]{2,0,1:T(8,128)(2,1)}), bf16[256,1,1024]{2,0,1:T(8,128)(2,1)}) %reduce-scatter.29.cloned.1.call-update) | async-done | bytes 524304 | tf_op jit(solution)/shard_map/reduce_scatter | solution.py:195
  1032.1 6.6 fusion.93
  1040.4 6.0 fusion.86
  1048.0 6.1 fusion.103
  1055.6 5.9 fusion.117
  1065.2 12.3 all-gather.37.cloned.1.call-done
  1085.8 45.2 %while.113 = (s32[]{:T(128)}, f32[4,1024,64]{1,2,0:T(8,128)}, f32[4,1024,64]{1,2,0:T(8,128)S(1)}, bf16[4,1024,64]{1,2,0:T(8,128)(2,1)S(1)}, bf16[4,1024,64]{2,1,...) while((s32[]{:T(128)}, f32[4,1024,64]{1,2,0:T(8,128)}, ...), condition=%wide.region_42.43_spmd, body=%wide.region_38.42_spmd.sunk | while | flops 340098560 | bytes 21916056 | solution.py:147
  1161.3 24.7 %reduce-scatter.45.cloned.1.call-done = f32[1024,128]{1,0:T(8,128)} async-done(((f32[1024,1024]{1,0:T(8,128)}), f32[1024,128]{1,0:T(8,128)}) %reduce-scatter.45.cloned.1.call-update) | async-done | bytes 524304 | tf_op jit(solution)/shard_map/reduce_scatter | solution.py:338
  1188.3 52.6 %reduce-scatter.43.cloned.1.call-done = f32[128,1024]{1,0:T(8,128)} async-done(((f32[1024,1024]{1,0:T(8,128)}), f32[128,1024]{1,0:T(8,128)}) %reduce-scatter.43.cloned.1.call-update) | async-done | bytes 524304 | tf_op jit(solution)/shard_map/reduce_scatter | solution.py:337
  1240.9 54.7 %reduce-scatter.41.cloned.1.call-done = f32[128,1024]{1,0:T(8,128)} async-done(((f32[1024,1024]{1,0:T(8,128)}), f32[128,1024]{1,0:T(8,128)}) %reduce-scatter.41.cloned.1.call-update) | async-done | bytes 524304 | tf_op jit(solution)/shard_map/reduce_scatter | solution.py:337
  1298.2 23.1 %all-reduce.1 = (f32[2,3,256]{2,1,0:T(4,128)S(1)}, f32[2,1024]{1,0:T(2,128)}) all-reduce(f32[2,3,256]{2,1,0:T(4,128)S(1)} %pad_maximum_fusion.13, f32[2,1024]{1,0:T(2,128)S(1)} %pad_maximum_fusion.14), channel_id=1, replica_groups=mesh['dp'=8,'tensor'=4] {'dp'}, use_global_device_ids=true, to_apply=%region_50.51 | all-reduce | flops 3584 | bytes 28672 | tf_op jit(solution)/shard_map/psum | solution.py:348
  1321.8 13.2 reduce-scatter.39.cloned.1.call-done
  1335.0 39.4 %reduce-scatter.37.cloned.1.call-done = f32[256,128]{1,0:T(8,128)} async-done(((f32[256,1024]{1,0:T(8,128)}), f32[256,128]{1,0:T(8,128)}) %reduce-scatter.37.cloned.1.call-update) | async-done | bytes 131088 | tf_op jit(solution)/shard_map/reduce_scatter | solution.py:336
  1376.1 44.6 %reduce-scatter.31.cloned.1.call-done = bf16[256,1,1024]{2,0,1:T(8,128)(2,1)} async-done(((bf16[1024,1,1024]{2,0,1:T(8,128)(2,1)}), bf16[256,1,1024]{2,0,1:T(8,128)(2,1)}) %reduce-scatter.31.cloned.1.call-update) | async-done | bytes 524304 | tf_op jit(solution)/shard_map/reduce_scatter | solution.py:195
  1426.0 40.6 %all-reduce = (f32[2,2,1024]{2,1,0:T(2,128)}, f32[2,2,1024]{2,1,0:T(2,128)}, f32[2,2,1024]{2,1,0:T(2,128)}) all-reduce(f32[2,2,1024]{2,1,0:T(2,128)S(1)} %pad_maximum_fusion.10, f32[2,2,1024]{2,1,0:T(2,128)S(1)} %pad_maximum_fusion.11, f32[2,2,1024]{2,1,0:T(2,128)S(1)} %pad_maximum_fusion.12), channel_id=1, replica_groups=mesh['dp'=8,'tensor'=4] {'dp','tensor'}, use_global_device_ids=true, to_apply=%region_64.65 | all-reduce | flops 12288 | bytes 98304 | tf_op jit(solution)/shard_map/psum | solution.py:345
  1470.0 49.8 %reduce-scatter.33.cloned.1.call-done = f32[128,3,256]{2,0,1:T(8,128)} async-done(((f32[1024,3,256]{2,0,1:T(8,128)}), f32[128,3,256]{2,0,1:T(8,128)}) %reduce-scatter.33.cloned.1.call-update) | async-done | bytes 393232 | tf_op jit(solution)/shard_map/reduce_scatter | solution.py:335
  (815 shorter events, 387.8 us)
Async XLA Ops:
  7.2 32.5 %all-gather.39.cloned.1.call-start = ((), (), s32[]{:S(2)}) async-start(), calls=%async_computation.40 | async-start | bytes 1769472 | tf_op jit(solution)/shard_map/all_gather | solution.py:206
  9.9 77.9 %all-gather.23.cloned.1.call-start = ((), (), s32[]{:S(2)}) async-start(), calls=%async_computation.16 | async-start | bytes 2621440 | tf_op jit(solution)/shard_map/all_gather | solution.py:173
  11.1 80.6 %copy-start.71 = (f32[256]{0:T(256)}, f32[256]{0:T(256)S(1)}, u32[]{:S(2)}) copy-start(f32[256]{0:T(256)S(1)} %broadcast_multiply_fusion.11) | copy-start | bytes 3076
  14.5 173.9 %copy-start.66 = (f32[1,1,1024]{2,1,0:T(1,128)}, f32[1,1,1024]{2,1,0:T(1,128)S(1)}, u32[]{:S(2)}) copy-start(f32[1,1,1024]{2,1,0:T(1,128)S(1)} %get-tuple-element.803) | copy-start | bytes 12292
  17.3 168.5 %reduce-scatter.17.cloned.1.call-start = ((), (), s32[]{:S(2)}) async-start(), calls=%async_computation.17 | async-start | bytes 2621440 | tf_op jit(solution)/shard_map/reduce_scatter | solution.py:183
  32.4 391.7 %copy-start.16 = (f32[1024,10]{0,1:T(8,128)}, f32[1024,10]{0,1:T(8,128)S(1)}, u32[]{:S(2)}) copy-start(f32[1024,10]{0,1:T(8,128)S(1)} %get-tuple-element.805) | copy-start | bytes 122884
  32.4 391.7 %copy-start.19 = (f32[1024,10]{0,1:T(8,128)}, f32[1024,10]{0,1:T(8,128)S(1)}, u32[]{:S(2)}) copy-start(f32[1024,10]{0,1:T(8,128)S(1)} %get-tuple-element.806) | copy-start | bytes 122884
  32.4 391.7 %copy-start.22 = (f32[1024,10]{0,1:T(8,128)}, f32[1024,10]{0,1:T(8,128)S(1)}, u32[]{:S(2)}) copy-start(f32[1024,10]{0,1:T(8,128)S(1)} %get-tuple-element.807) | copy-start | bytes 122884
  143.0 72.5 %all-gather.41.cloned.1.call-start = ((), (), s32[]{:S(2)}) async-start(), calls=%async_computation.41 | async-start | bytes 2359296 | tf_op jit(solution)/shard_map/all_gather | solution.py:208
  144.9 118.6 %all-gather.25.cloned.1.call-start = ((), (), s32[]{:S(2)}) async-start(), calls=%async_computation.18 | async-start | bytes 2621440 | tf_op jit(solution)/shard_map/all_gather | solution.py:173
  145.6 197.3 %copy-start.57 = (f32[1,1,1024]{2,1,0:T(1,128)}, f32[1,1,1024]{2,1,0:T(1,128)S(1)}, u32[]{:S(2)}) copy-start(f32[1,1,1024]{2,1,0:T(1,128)S(1)} %get-tuple-element.800) | copy-start | bytes 12292
  187.1 90.9 %copy-start.73 = (f32[256]{0:T(256)}, f32[256]{0:T(256)S(1)}, u32[]{:S(2)}) copy-start(f32[256]{0:T(256)S(1)} %broadcast_multiply_fusion.10) | copy-start | bytes 3076
  188.4 89.5 %copy-start.93 = (f32[256]{0:T(256)}, f32[256]{0:T(256)S(1)}, u32[]{:S(2)}) copy-start(f32[256]{0:T(256)S(1)} %add_rsqrt_fusion.2) | copy-start | bytes 3076
  190.6 102.3 %all-gather.43.cloned.1.call-start = ((), (), s32[]{:S(2)}) async-start(), calls=%async_computation.42 | async-start | bytes 2359296 | tf_op jit(solution)/shard_map/all_gather | solution.py:209
  192.6 150.4 %reduce-scatter.19.cloned.1.call-start = ((), (), s32[]{:S(2)}) async-start(), calls=%async_computation.19 | async-start | bytes 2621440 | tf_op jit(solution)/shard_map/reduce_scatter | solution.py:183
  193.5 84.5 %copy-start.100 = (f32[1,1024]{1,0:T(1,128)}, f32[1,1024]{1,0:T(1,128)S(1)}, u32[]{:S(2)}) copy-start(f32[1,1024]{1,0:T(1,128)S(1)} %get-tuple-element.788) | copy-start | bytes 12292
  298.9 71.7 %all-gather.45.cloned.1.call-start = ((), (), s32[]{:S(2)}) async-start(), calls=%async_computation.43 | async-start | bytes 1769472 | tf_op jit(solution)/shard_map/all_gather | solution.py:206
  299.8 118.9 %all-gather.27.cloned.1.call-start = ((), (), s32[]{:S(2)}) async-start(), calls=%async_computation.20 | async-start | bytes 2621440 | tf_op jit(solution)/shard_map/all_gather | solution.py:173
  344.3 165.2 %copy-start.3 = (f32[256,1,1024]{2,0,1:T(8,128)}, f32[256,1,1024]{2,0,1:T(8,128)S(1)}, u32[]{:S(2)}) copy-start(f32[256,1,1024]{2,0,1:T(8,128)S(1)} %get-tuple-element.646) | copy-start | bytes 3145732
  345.7 163.8 %reduce-scatter.21.cloned.1.call-start = ((), (), s32[]{:S(2)}) async-start(), calls=%async_computation.21 | async-start | bytes 2621440 | tf_op jit(solution)/shard_map/reduce_scatter | solution.py:183
  466.8 72.6 %all-gather.47.cloned.1.call-start = ((), (), s32[]{:S(2)}) async-start(), calls=%async_computation.44 | async-start | bytes 2359296 | tf_op jit(solution)/shard_map/all_gather | solution.py:208
  467.5 119.9 %all-gather.29.cloned.1.call-start = ((), (), s32[]{:S(2)}) async-start(), calls=%async_computation.22 | async-start | bytes 2621440 | tf_op jit(solution)/shard_map/all_gather | solution.py:173
  512.2 121.5 %all-gather.31.cloned.1.call-start = ((), (), s32[]{:S(2)}) async-start(), calls=%async_computation.24 | async-start | bytes 2621440 | tf_op jit(solution)/shard_map/all_gather | solution.py:176
  514.4 148.2 %all-gather.49.cloned.1.call-start = ((), (), s32[]{:S(2)}) async-start(), calls=%async_computation.45 | async-start | bytes 2359296 | tf_op jit(solution)/shard_map/all_gather | solution.py:209
  515.0 203.9 %reduce-scatter.25.cloned.1.call-start = ((), (), s32[]{:S(2)}) async-start(), calls=%async_computation.25 | async-start | bytes 2621440 | tf_op jit(solution)/shard_map/reduce_scatter | solution.py:195
  674.9 89.4 %reduce-scatter.23.cloned.1.call-start = ((), (), s32[]{:S(2)}) async-start(), calls=%async_computation.23 | async-start | bytes 2621440 | tf_op jit(solution)/shard_map/reduce_scatter | solution.py:183
  680.8 83.5 %copy-start.92 = (f32[1,1,1024]{2,1,0:T(1,128)S(1)}, f32[1,1,1024]{2,1,0:T(1,128)}, u32[]{:S(2)}) copy-start(f32[1,1,1024]{2,1,0:T(1,128)} %get-tuple-element.769) | copy-start | bytes 12292
  680.8 132.8 %all-gather.33.cloned.1.call-start = ((), (), s32[]{:S(2)}) async-start(), calls=%async_computation.26 | async-start | bytes 2621440 | tf_op jit(solution)/shard_map/all_gather | solution.py:176
  768.3 152.5 %reduce-scatter.27.cloned.1.call-start = ((), (), s32[]{:S(2)}) async-start(), calls=%async_computation.27 | async-start | bytes 2621440 | tf_op jit(solution)/shard_map/reduce_scatter | solution.py:195
  878.0 93.2 %copy-start.101 = (f32[1,1024]{1,0:T(1,128)S(1)}, f32[1,1024]{1,0:T(1,128)}, u32[]{:S(2)}) copy-start(f32[1,1024]{1,0:T(1,128)} %copy-done.100) | copy-start | bytes 12292
  878.0 93.2 %all-gather.35.cloned.1.call-start = ((), (), s32[]{:S(2)}) async-start(), calls=%async_computation.28 | async-start | bytes 2621440 | tf_op jit(solution)/shard_map/all_gather | solution.py:176
  925.8 100.6 %reduce-scatter.29.cloned.1.call-start = ((), (), s32[]{:S(2)}) async-start(), calls=%async_computation.29 | async-start | bytes 2621440 | tf_op jit(solution)/shard_map/reduce_scatter | solution.py:195
  983.7 93.8 %all-gather.37.cloned.1.call-start = ((), (), s32[]{:S(2)}) async-start(), calls=%async_computation.30 | async-start | bytes 2621440 | tf_op jit(solution)/shard_map/all_gather | solution.py:176
  1032.0 129.2 %reduce-scatter.47.cloned.1.call-start = ((), (), s32[]{:S(2)}) async-start(), calls=%async_computation.39 | async-start | bytes 4718592 | tf_op jit(solution)/shard_map/reduce_scatter | solution.py:338
  1038.7 147.2 %reduce-scatter.45.cloned.1.call-start = ((), (), s32[]{:S(2)}) async-start(), calls=%async_computation.38 | async-start | bytes 4718592 | tf_op jit(solution)/shard_map/reduce_scatter | solution.py:338
  1046.4 194.5 %reduce-scatter.43.cloned.1.call-start = ((), (), s32[]{:S(2)}) async-start(), calls=%async_computation.37 | async-start | bytes 4718592 | tf_op jit(solution)/shard_map/reduce_scatter | solution.py:337
  1054.1 241.5 %reduce-scatter.41.cloned.1.call-start = ((), (), s32[]{:S(2)}) async-start(), calls=%async_computation.36 | async-start | bytes 4718592 | tf_op jit(solution)/shard_map/reduce_scatter | solution.py:337
  1061.6 273.4 %reduce-scatter.39.cloned.1.call-start = ((), (), s32[]{:S(2)}) async-start(), calls=%async_computation.35 | async-start | bytes 1179648 | tf_op jit(solution)/shard_map/reduce_scatter | solution.py:336
  1065.1 309.4 %reduce-scatter.37.cloned.1.call-start = ((), (), s32[]{:S(2)}) async-start(), calls=%async_computation.34 | async-start | bytes 1179648 | tf_op jit(solution)/shard_map/reduce_scatter | solution.py:336
  1084.5 336.2 %reduce-scatter.31.cloned.1.call-start = ((), (), s32[]{:S(2)}) async-start(), calls=%async_computation.31 | async-start | bytes 2621440 | tf_op jit(solution)/shard_map/reduce_scatter | solution.py:195
  1145.1 324.9 %reduce-scatter.35.cloned.1.call-start = ((), (), s32[]{:S(2)}) async-start(), calls=%async_computation.33 | async-start | bytes 3538944 | tf_op jit(solution)/shard_map/reduce_scatter | solution.py:335
  1150.7 369.1 %reduce-scatter.33.cloned.1.call-start = ((), (), s32[]{:S(2)}) async-start(), calls=%async_computation.32 | async-start | bytes 3538944 | tf_op jit(solution)/shard_map/reduce_scatter | solution.py:335
  1160.7 137.2 %copy-start.29 = (bf16[1024,1,4,64]{0,3,2,1:T(8,128)(2,1)S(1)}, bf16[1024,1,4,64]{0,3,2,1:T(8,128)(2,1)}, u32[]{:S(2)}) copy-start(bf16[1024,1,4,64]{0,3,2,1:T(8,128)(2,1)} %copy-done.28) | copy-start | bytes 1572868
  1186.0 234.8 %copy-start.2 = (bf16[256,1,1024]{2,0,1:T(8,128)(2,1)S(1)}, bf16[256,1,1024]{2,0,1:T(8,128)(2,1)}, u32[]{:S(2)}) copy-start(bf16[256,1,1024]{2,0,1:T(8,128)(2,1)} %param.29) | copy-start | bytes 1572868
  1186.0 234.8 %copy-start.63 = (f32[1,1,1024]{2,1,0:T(1,128)S(1)}, f32[1,1,1024]{2,1,0:T(1,128)}, u32[]{:S(2)}) copy-start(f32[1,1,1024]{2,1,0:T(1,128)} %copy-done.62) | copy-start | bytes 12292
  1186.0 234.8 %copy-start.72 = (f32[256]{0:T(256)S(1)}, f32[256]{0:T(256)}, u32[]{:S(2)}) copy-start(f32[256]{0:T(256)} %copy-done.71) | copy-start | bytes 3076
  1186.0 234.8 %copy-start.89 = (f32[256]{0:T(256)S(1)}, f32[256]{0:T(256)}, u32[]{:S(2)}) copy-start(f32[256]{0:T(256)} %copy-done.88) | copy-start | bytes 3076
  1188.3 234.1 %copy-start.33 = (f32[256,1,1024]{2,0,1:T(8,128)S(1)}, f32[256,1,1024]{2,0,1:T(8,128)}, u32[]{:S(2)}) copy-start(f32[256,1,1024]{2,0,1:T(8,128)} %get-tuple-element.634) | copy-start | bytes 3145732
  (95 other events, 2122.7 us)
Sparse Core Ops, SparseCore 0:
  10.5 29.1 all-gather.38
  41.8 45.9 all-gather.22
  143.1 42.5 reduce-scatter.16
  188.2 27.1 all-gather.40
  217.5 45.9 all-gather.24
  266.0 26.9 all-gather.42
  299.0 43.8 reduce-scatter.18
  345.4 25.1 all-gather.44
  372.8 45.9 all-gather.26
  466.9 42.5 reduce-scatter.20
  512.2 27.1 all-gather.46
  541.5 45.9 all-gather.28
  589.1 44.5 all-gather.30
  635.6 26.9 all-gather.48
  675.0 43.8 reduce-scatter.24
  721.0 43.1 reduce-scatter.22
  768.4 45.2 all-gather.32
  878.2 42.5 reduce-scatter.26
  926.0 45.2 all-gather.34
  983.8 42.5 reduce-scatter.28
  1032.1 45.2 all-gather.36
  1081.1 50.0 reduce-scatter.46
  1134.6 51.2 reduce-scatter.44
  1189.5 51.3 reduce-scatter.42
  1244.3 51.2 reduce-scatter.40
  1298.9 36.0 reduce-scatter.38
  1338.4 36.0 reduce-scatter.36
  1376.8 43.8 reduce-scatter.30
  1424.1 45.8 reduce-scatter.34
  1473.6 46.1 reduce-scatter.32
where the time goes:
time: 1540 us; the launch traced here: 1530 us
  waiting for transfers between devices  1010 us (66%)
  matrix products  190 us (12%)
  local copies, waits for them, and re-layouts  148 us (10%)
  blocking collectives  89.3 us (6%)
  other arithmetic  69.1 us (4%)
  between operations  16.8 us (1%)
    all_gather x4, waiting for transfers between devices, spread_rows(): return lax.all_gather(normed, 'tensor', axis=0, tiled=True)  192 us
    reduce_scatter x4, waiting for transfers between devices, collect_rows(): lax.psum_scatter(partial_term(jnp.int32(0), row_count * lax.axis_size('te...  168 us
    reduce_scatter x4, waiting for transfers between devices, collect_grads(): lax.psum_scatter(partial_term(jnp.int32(0), row_count * lax.axis_size('te...  168 us
    all_gather x4, waiting for transfers between devices, spread_grads(): return lax.all_gather(upstream_low, 'tensor', axis=0, tiled=True)  133 us
    reduce_scatter x2, waiting for transfers between devices, shards(): lax.psum_scatter(expand_grad, 'dp', scatter_dimension=0, tiled=True)  107 us
    reduce_scatter x2, waiting for transfers between devices, shards(): lax.psum_scatter(triple_grad, 'dp', scatter_dimension=0, tiled=True)  53.3 us
    reduce_scatter x2, waiting for transfers between devices, shards(): lax.psum_scatter(exit_grad, 'dp', scatter_dimension=1, tiled=True)  52.6 us
    all_gather x2, waiting for transfers between devices, shards(): lax.all_gather(expand_weight[layer_index], 'dp', axis=0, tiled=True)  46.1 us
  transfers between devices with their start and end apart: 30, of which 29 were waited for; matrix products, arithmetic and copies ran while one was open for 12% of the time, Pallas kernels for 0%

commit v1 on v0

--- a/solution.py
+++ b/solution.py
@@ -343,7 +343,8 @@
     ]
     triple_total, exit_total, expand_total, shrink_total = stacked
     gain_total, shift_total, bias_total = lax.psum(
-        (jnp.stack(gain_parts), jnp.stack(shift_parts), jnp.stack(bias_parts)), ("dp", "tensor")
+        lax.psum((jnp.stack(gain_parts), jnp.stack(shift_parts), jnp.stack(bias_parts)), "tensor"),
+        "dp",
     )
     triple_bias_total, expand_bias_total = lax.psum(
         (jnp.stack(triple_bias_parts), jnp.stack(expand_bias_parts)), "dp"

time: 1540 us -> 1540 us (level)
  blocking collectives: 89.3 us -> 67.4 us
  waiting for transfers between devices: 1010 us -> 1030 us
    reduce_scatter x2, waiting for transfers between devices: 52.6 us -> 76.3 us  [shards(): lax.psum_scatter(exit_grad, 'dp', scatter_dimension=1, tiled=True)]
    psum x1, blocking collectives: 40.6 us -> 17.6 us  [shards(): lax.psum((jnp.stack(gain_parts), jnp.stack(shift_parts), jnp.stack(bias_p...]
where the time goes in v1:
time: 1540 us; the launch traced here: 1530 us
  waiting for transfers between devices  1030 us (67%)
  matrix products  190 us (12%)
  local copies, waits for them, and re-layouts  148 us (10%)
  other arithmetic  69.1 us (4%)
  blocking collectives  67.4 us (4%)
  between operations  16.8 us (1%)
    all_gather x4, waiting for transfers between devices, spread_rows(): return lax.all_gather(normed, 'tensor', axis=0, tiled=True)  192 us
    reduce_scatter x4, waiting for transfers between devices, collect_rows(): lax.psum_scatter(partial_term(jnp.int32(0), row_count * lax.axis_size('te...  168 us
    reduce_scatter x4, waiting for transfers between devices, collect_grads(): lax.psum_scatter(partial_term(jnp.int32(0), row_count * lax.axis_size('te...  168 us
    all_gather x4, waiting for transfers between devices, spread_grads(): return lax.all_gather(upstream_low, 'tensor', axis=0, tiled=True)  133 us
    reduce_scatter x2, waiting for transfers between devices, shards(): lax.psum_scatter(expand_grad, 'dp', scatter_dimension=0, tiled=True)  107 us
    reduce_scatter x2, waiting for transfers between devices, shards(): lax.psum_scatter(exit_grad, 'dp', scatter_dimension=1, tiled=True)  76.3 us
    reduce_scatter x2, waiting for transfers between devices, shards(): lax.psum_scatter(triple_grad, 'dp', scatter_dimension=0, tiled=True)  51.8 us
    all_gather x2, waiting for transfers between devices, shards(): lax.all_gather(expand_weight[layer_index], 'dp', axis=0, tiled=True)  46.1 us
  transfers between devices with their start and end apart: 30, of which 29 were waited for; matrix products, arithmetic and copies ran while one was open for 12% of the time, Pallas kernels for 0%

profile of v1, /device:TPU:0, one launch (start us, length us, event | category | flops | bytes accessed | tf_op | source)
XLA Modules:
  0.0 1529.2 jit_solution(1203030126719709577)
XLA Ops:
  18.6 13.0 all-gather.1
  32.4 7.3 all-gather.39.cloned.1.call-done
  39.7 48.1 %all-gather.23.cloned.1.call-done = bf16[1024,1,1024]{2,0,1:T(8,128)(2,1)} async-done(((bf16[256,1,1024]{2,0,1:T(8,128)(2,1)}), bf16[1024,1,1024]{2,0,1:T(8,128)(2,1)}) %all-gather.23.cloned.1.call-update) | async-done | bytes 2097168 | tf_op jit(solution)/shard_map/all_gather | solution.py:173
  94.5 12.1 concatenate.87
  110.9 28.1 %while.107 = (s32[]{:T(128)}, bf16[4,1024,64]{1,2,0:T(8,128)(2,1)}, f32[4,1024]{1,0:T(4,128)}, bf16[4,1024,64]{2,1,0:T(8,128)(2,1)S(1)}, bf16[4,1024,64]{2,1,0:T...) while((s32[]{:T(128)}, bf16[4,1024,64]{1,2,0:T(8,128)(2,1)}, ...), condition=%wide.region_7.8_spmd, body=%wide.region_2.7_spmd.sunk | while | flops 138968576 | bytes 8622382 | solution.py:96
  145.6 40.1 %reduce-scatter.17.cloned.1.call-done = bf16[256,1,1024]{2,0,1:T(8,128)(2,1)} async-done(((bf16[1024,1,1024]{2,0,1:T(8,128)(2,1)}), bf16[256,1,1024]{2,0,1:T(8,128)(2,1)}) %reduce-scatter.17.cloned.1.call-update) | async-done | bytes 524304 | tf_op jit(solution)/shard_map/reduce_scatter | solution.py:183
  193.5 22.0 %all-gather.41.cloned.1.call-done = bf16[1,1024,1024]{2,1,0:T(8,128)(2,1)} async-done(((bf16[1,128,1024]{2,1,0:T(8,128)(2,1)}), bf16[1,1024,1024]{2,1,0:T(8,128)(2,1)}) %all-gather.41.cloned.1.call-update) | async-done | bytes 2097168 | tf_op jit(solution)/shard_map/all_gather | solution.py:208
  215.5 48.0 %all-gather.25.cloned.1.call-done = bf16[1024,1,1024]{2,0,1:T(8,128)(2,1)} async-done(((bf16[256,1,1024]{2,0,1:T(8,128)(2,1)}), bf16[1024,1,1024]{2,0,1:T(8,128)(2,1)}) %all-gather.25.cloned.1.call-update) | async-done | bytes 2097168 | tf_op jit(solution)/shard_map/all_gather | solution.py:173
  263.5 14.5 fusion.52
  278.0 14.9 all-gather.43.cloned.1.call-done
  292.9 6.0 convert_bitcast_fusion.4
  299.9 43.1 %reduce-scatter.19.cloned.1.call-done = bf16[256,1,1024]{2,0,1:T(8,128)(2,1)} async-done(((bf16[1024,1,1024]{2,0,1:T(8,128)(2,1)}), bf16[256,1,1024]{2,0,1:T(8,128)(2,1)}) %reduce-scatter.19.cloned.1.call-update) | async-done | bytes 524304 | tf_op jit(solution)/shard_map/reduce_scatter | solution.py:183
  345.8 12.7 all-gather.5
  358.5 12.1 all-gather.45.cloned.1.call-done
  370.6 48.1 %all-gather.27.cloned.1.call-done = bf16[1024,1,1024]{2,0,1:T(8,128)(2,1)} async-done(((bf16[256,1,1024]{2,0,1:T(8,128)(2,1)}), bf16[1024,1,1024]{2,0,1:T(8,128)(2,1)}) %all-gather.27.cloned.1.call-update) | async-done | bytes 2097168 | tf_op jit(solution)/shard_map/all_gather | solution.py:173
  426.2 7.8 concatenate.89
  437.2 26.0 %while.109 = (s32[]{:T(128)}, bf16[4,1024,64]{1,2,0:T(8,128)(2,1)S(1)}, f32[4,1024]{1,0:T(4,128)}, bf16[4,1024,64]{2,1,0:T(8,128)(2,1)S(1)}, bf16[4,1024,64]{2,1...) while((s32[]{:T(128)}, ...), condition=%wide.region_19.20_spmd, body=%wide.region_14.19_spmd.sunk | while | flops 138968576 | bytes 8622382 | solution.py:96
  467.6 42.0 %reduce-scatter.21.cloned.1.call-done = bf16[256,1,1024]{2,0,1:T(8,128)(2,1)} async-done(((bf16[1024,1,1024]{2,0,1:T(8,128)(2,1)}), bf16[256,1,1024]{2,0,1:T(8,128)(2,1)}) %reduce-scatter.21.cloned.1.call-update) | async-done | bytes 524304 | tf_op jit(solution)/shard_map/reduce_scatter | solution.py:183
  515.2 24.2 %all-gather.47.cloned.1.call-done = bf16[1,1024,1024]{2,1,0:T(8,128)(2,1)} async-done(((bf16[1,128,1024]{2,1,0:T(8,128)(2,1)}), bf16[1,1024,1024]{2,1,0:T(8,128)(2,1)}) %all-gather.47.cloned.1.call-update) | async-done | bytes 2097168 | tf_op jit(solution)/shard_map/all_gather | solution.py:208
  539.4 48.0 %all-gather.29.cloned.1.call-done = bf16[1024,1,1024]{2,0,1:T(8,128)(2,1)} async-done(((bf16[256,1,1024]{2,0,1:T(8,128)(2,1)}), bf16[1024,1,1024]{2,0,1:T(8,128)(2,1)}) %all-gather.29.cloned.1.call-update) | async-done | bytes 2097168 | tf_op jit(solution)/shard_map/all_gather | solution.py:173
  587.4 14.5 fusion.55
  602.0 31.7 %all-gather.31.cloned.1.call-done = bf16[1024,1,1024]{2,0,1:T(8,128)(2,1)} async-done(((bf16[256,1,1024]{2,0,1:T(8,128)(2,1)}), bf16[1024,1,1024]{2,0,1:T(8,128)(2,1)}) %all-gather.31.cloned.1.call-update) | async-done | bytes 2097168 | tf_op jit(solution)/shard_map/all_gather | solution.py:176
  633.7 28.9 %all-gather.49.cloned.1.call-done = bf16[1,1024,1024]{2,1,0:T(8,128)(2,1)} async-done(((bf16[1,1024,128]{2,1,0:T(8,128)(2,1)}), bf16[1,1024,1024]{2,1,0:T(8,128)(2,1)}) %all-gather.49.cloned.1.call-update) | async-done | bytes 2097168 | tf_op jit(solution)/shard_map/all_gather | solution.py:209
  662.6 7.2 convert_reduce_fusion
  674.9 5.9 convert_bitcast_fusion.2
  680.9 38.0 %reduce-scatter.25.cloned.1.call-done = bf16[256,1,1024]{2,0,1:T(8,128)(2,1)} async-done(((bf16[1024,1,1024]{2,0,1:T(8,128)(2,1)}), bf16[256,1,1024]{2,0,1:T(8,128)(2,1)}) %reduce-scatter.25.cloned.1.call-update) | async-done | bytes 524304 | tf_op jit(solution)/shard_map/reduce_scatter | solution.py:195
  721.0 43.2 %reduce-scatter.23.cloned.1.call-done = bf16[256,1,1024]{2,0,1:T(8,128)(2,1)} async-done(((bf16[1024,1,1024]{2,0,1:T(8,128)(2,1)}), bf16[256,1,1024]{2,0,1:T(8,128)(2,1)}) %reduce-scatter.23.cloned.1.call-update) | async-done | bytes 524304 | tf_op jit(solution)/shard_map/reduce_scatter | solution.py:183
  770.0 43.6 %all-gather.33.cloned.1.call-done = bf16[1024,1,1024]{2,0,1:T(8,128)(2,1)} async-done(((bf16[256,1,1024]{2,0,1:T(8,128)(2,1)}), bf16[1024,1,1024]{2,0,1:T(8,128)(2,1)}) %all-gather.33.cloned.1.call-update) | async-done | bytes 2097168 | tf_op jit(solution)/shard_map/all_gather | solution.py:176
  818.6 45.1 %while.111 = (s32[]{:T(128)}, f32[4,1024,64]{1,2,0:T(8,128)}, f32[4,1024,64]{1,2,0:T(8,128)S(1)}, bf16[4,1024,64]{1,2,0:T(8,128)(2,1)S(1)}, bf16[4,1024,64]{2,1,...) while((s32[]{:T(128)}, f32[4,1024,64]{1,2,0:T(8,128)}, ...), condition=%wide.region_31.32_spmd, body=%wide.region_27.31_spmd.sunk | while | flops 340098560 | bytes 21916056 | solution.py:147
  878.1 42.7 %reduce-scatter.27.cloned.1.call-done = bf16[256,1,1024]{2,0,1:T(8,128)(2,1)} async-done(((bf16[1024,1,1024]{2,0,1:T(8,128)(2,1)}), bf16[256,1,1024]{2,0,1:T(8,128)(2,1)}) %reduce-scatter.27.cloned.1.call-update) | async-done | bytes 524304 | tf_op jit(solution)/shard_map/reduce_scatter | solution.py:195
  926.3 45.0 %all-gather.35.cloned.1.call-done = bf16[1024,1,1024]{2,0,1:T(8,128)(2,1)} async-done(((bf16[256,1,1024]{2,0,1:T(8,128)(2,1)}), bf16[1024,1,1024]{2,0,1:T(8,128)(2,1)}) %all-gather.35.cloned.1.call-update) | async-done | bytes 2097168 | tf_op jit(solution)/shard_map/all_gather | solution.py:176
  971.3 7.2 convert_reduce_fusion.1
  983.7 42.7 %reduce-scatter.29.cloned.1.call-done = bf16[256,1,1024]{2,0,1:T(8,128)(2,1)} async-done(((bf16[1024,1,1024]{2,0,1:T(8,128)(2,1)}), bf16[256,1,1024]{2,0,1:T(8,128)(2,1)}) %reduce-scatter.29.cloned.1.call-update) | async-done | bytes 524304 | tf_op jit(solution)/shard_map/reduce_scatter | solution.py:195
  1032.1 6.6 fusion.93
  1040.4 6.0 fusion.86
  1048.0 6.1 fusion.103
  1055.6 5.9 fusion.117
  1065.2 12.3 all-gather.37.cloned.1.call-done
  1085.8 45.2 %while.113 = (s32[]{:T(128)}, f32[4,1024,64]{1,2,0:T(8,128)}, f32[4,1024,64]{1,2,0:T(8,128)S(1)}, bf16[4,1024,64]{1,2,0:T(8,128)(2,1)S(1)}, bf16[4,1024,64]{2,1,...) while((s32[]{:T(128)}, f32[4,1024,64]{1,2,0:T(8,128)}, ...), condition=%wide.region_42.43_spmd, body=%wide.region_38.42_spmd.sunk | while | flops 340098560 | bytes 21916056 | solution.py:147
  1161.3 24.7 %reduce-scatter.45.cloned.1.call-done = f32[1024,128]{1,0:T(8,128)} async-done(((f32[1024,1024]{1,0:T(8,128)}), f32[1024,128]{1,0:T(8,128)}) %reduce-scatter.45.cloned.1.call-update) | async-done | bytes 524304 | tf_op jit(solution)/shard_map/reduce_scatter | solution.py:338
  1188.3 52.6 %reduce-scatter.43.cloned.1.call-done = f32[128,1024]{1,0:T(8,128)} async-done(((f32[1024,1024]{1,0:T(8,128)}), f32[128,1024]{1,0:T(8,128)}) %reduce-scatter.43.cloned.1.call-update) | async-done | bytes 524304 | tf_op jit(solution)/shard_map/reduce_scatter | solution.py:337
  1240.9 54.7 %reduce-scatter.41.cloned.1.call-done = f32[128,1024]{1,0:T(8,128)} async-done(((f32[1024,1024]{1,0:T(8,128)}), f32[128,1024]{1,0:T(8,128)}) %reduce-scatter.41.cloned.1.call-update) | async-done | bytes 524304 | tf_op jit(solution)/shard_map/reduce_scatter | solution.py:337
  1298.2 36.9 %reduce-scatter.39.cloned.1.call-done = f32[256,128]{1,0:T(8,128)} async-done(((f32[256,1024]{1,0:T(8,128)}), f32[256,128]{1,0:T(8,128)}) %reduce-scatter.39.cloned.1.call-update) | async-done | bytes 131088 | tf_op jit(solution)/shard_map/reduce_scatter | solution.py:336
  1335.0 39.4 %reduce-scatter.37.cloned.1.call-done = f32[256,128]{1,0:T(8,128)} async-done(((f32[256,1024]{1,0:T(8,128)}), f32[256,128]{1,0:T(8,128)}) %reduce-scatter.37.cloned.1.call-update) | async-done | bytes 131088 | tf_op jit(solution)/shard_map/reduce_scatter | solution.py:336
  1376.1 44.6 %reduce-scatter.31.cloned.1.call-done = bf16[256,1,1024]{2,0,1:T(8,128)(2,1)} async-done(((bf16[1024,1,1024]{2,0,1:T(8,128)(2,1)}), bf16[256,1,1024]{2,0,1:T(8,128)(2,1)}) %reduce-scatter.31.cloned.1.call-update) | async-done | bytes 524304 | tf_op jit(solution)/shard_map/reduce_scatter | solution.py:195
  1426.0 17.6 %all-reduce.1 = (f32[2,2,1024]{2,1,0:T(2,128)S(1)}, f32[2,2,1024]{2,1,0:T(2,128)S(1)}, f32[2,2,1024]{2,1,0:T(2,128)S(1)}) all-reduce(f32[2,2,1024]{2,1,0:T(2,128)S(1)} %pad_maximum_fusion.10, f32[2,2,1024]{2,1,0:T(2,128)S(1)} %pad_maximum_fusion.11, ...), channel_id=1, replica_groups=mesh['dp'=8,'tensor'=4] {'tensor'}, use_global_device_ids=true, to_apply=%region_64.65 | all-reduce | flops 12288 | bytes 98304 | tf_op jit(solution)/shard_map/psum | solution.py:346
  1443.5 24.1 %all-reduce = (f32[2,3,256]{2,1,0:T(4,128)S(1)}, f32[2,1024]{1,0:T(2,128)}, f32[2,2,1024]{2,1,0:T(2,128)}, f32[2,2,1024]{2,1,0:T(2,128)}, f32[2,2,1024]{2,1,0:T(2,128)}) all-reduce(f32[2,3,256]{2,1,0:T(4,128)S(1)} %pad_maximum_fusion.13, f32[2,1024]{1,0:T(2,128)S(1)} %pad_maximum_fusion.14, ...), channel_id=1, replica_groups=mesh['dp'=8,'tensor'=4] {'dp'}, use_global_device_ids=true, to_apply=%region_50.51 | all-reduce | flops 15872 | bytes 126976 | tf_op jit(solution)/shard_map/psum | solution.py:349
  1470.2 49.8 %reduce-scatter.33.cloned.1.call-done = f32[128,3,256]{2,0,1:T(8,128)} async-done(((f32[1024,3,256]{2,0,1:T(8,128)}), f32[128,3,256]{2,0,1:T(8,128)}) %reduce-scatter.33.cloned.1.call-update) | async-done | bytes 393232 | tf_op jit(solution)/shard_map/reduce_scatter | solution.py:335
  (815 shorter events, 386.2 us)
Async XLA Ops:
  7.2 32.5 %all-gather.39.cloned.1.call-start = ((), (), s32[]{:S(2)}) async-start(), calls=%async_computation.40 | async-start | bytes 1769472 | tf_op jit(solution)/shard_map/all_gather | solution.py:206
  9.9 77.9 %all-gather.23.cloned.1.call-start = ((), (), s32[]{:S(2)}) async-start(), calls=%async_computation.16 | async-start | bytes 2621440 | tf_op jit(solution)/shard_map/all_gather | solution.py:173
  11.1 80.6 %copy-start.71 = (f32[256]{0:T(256)}, f32[256]{0:T(256)S(1)}, u32[]{:S(2)}) copy-start(f32[256]{0:T(256)S(1)} %broadcast_multiply_fusion.11) | copy-start | bytes 3076
  14.5 173.9 %copy-start.66 = (f32[1,1,1024]{2,1,0:T(1,128)}, f32[1,1,1024]{2,1,0:T(1,128)S(1)}, u32[]{:S(2)}) copy-start(f32[1,1,1024]{2,1,0:T(1,128)S(1)} %get-tuple-element.806) | copy-start | bytes 12292
  17.3 168.5 %reduce-scatter.17.cloned.1.call-start = ((), (), s32[]{:S(2)}) async-start(), calls=%async_computation.17 | async-start | bytes 2621440 | tf_op jit(solution)/shard_map/reduce_scatter | solution.py:183
  32.4 391.7 %copy-start.16 = (f32[1024,10]{0,1:T(8,128)}, f32[1024,10]{0,1:T(8,128)S(1)}, u32[]{:S(2)}) copy-start(f32[1024,10]{0,1:T(8,128)S(1)} %get-tuple-element.808) | copy-start | bytes 122884
  32.4 391.7 %copy-start.19 = (f32[1024,10]{0,1:T(8,128)}, f32[1024,10]{0,1:T(8,128)S(1)}, u32[]{:S(2)}) copy-start(f32[1024,10]{0,1:T(8,128)S(1)} %get-tuple-element.809) | copy-start | bytes 122884
  32.4 391.7 %copy-start.22 = (f32[1024,10]{0,1:T(8,128)}, f32[1024,10]{0,1:T(8,128)S(1)}, u32[]{:S(2)}) copy-start(f32[1024,10]{0,1:T(8,128)S(1)} %get-tuple-element.810) | copy-start | bytes 122884
  143.0 72.5 %all-gather.41.cloned.1.call-start = ((), (), s32[]{:S(2)}) async-start(), calls=%async_computation.41 | async-start | bytes 2359296 | tf_op jit(solution)/shard_map/all_gather | solution.py:208
  144.9 118.6 %all-gather.25.cloned.1.call-start = ((), (), s32[]{:S(2)}) async-start(), calls=%async_computation.18 | async-start | bytes 2621440 | tf_op jit(solution)/shard_map/all_gather | solution.py:173
  145.6 197.3 %copy-start.57 = (f32[1,1,1024]{2,1,0:T(1,128)}, f32[1,1,1024]{2,1,0:T(1,128)S(1)}, u32[]{:S(2)}) copy-start(f32[1,1,1024]{2,1,0:T(1,128)S(1)} %get-tuple-element.803) | copy-start | bytes 12292
  187.1 90.9 %copy-start.73 = (f32[256]{0:T(256)}, f32[256]{0:T(256)S(1)}, u32[]{:S(2)}) copy-start(f32[256]{0:T(256)S(1)} %broadcast_multiply_fusion.10) | copy-start | bytes 3076
  188.4 89.5 %copy-start.93 = (f32[256]{0:T(256)}, f32[256]{0:T(256)S(1)}, u32[]{:S(2)}) copy-start(f32[256]{0:T(256)S(1)} %add_rsqrt_fusion.2) | copy-start | bytes 3076
  190.6 102.3 %all-gather.43.cloned.1.call-start = ((), (), s32[]{:S(2)}) async-start(), calls=%async_computation.42 | async-start | bytes 2359296 | tf_op jit(solution)/shard_map/all_gather | solution.py:209
  192.6 150.4 %reduce-scatter.19.cloned.1.call-start = ((), (), s32[]{:S(2)}) async-start(), calls=%async_computation.19 | async-start | bytes 2621440 | tf_op jit(solution)/shard_map/reduce_scatter | solution.py:183
  193.5 84.5 %copy-start.100 = (f32[1,1024]{1,0:T(1,128)}, f32[1,1024]{1,0:T(1,128)S(1)}, u32[]{:S(2)}) copy-start(f32[1,1024]{1,0:T(1,128)S(1)} %get-tuple-element.791) | copy-start | bytes 12292
  298.9 71.7 %all-gather.45.cloned.1.call-start = ((), (), s32[]{:S(2)}) async-start(), calls=%async_computation.43 | async-start | bytes 1769472 | tf_op jit(solution)/shard_map/all_gather | solution.py:206
  299.8 118.9 %all-gather.27.cloned.1.call-start = ((), (), s32[]{:S(2)}) async-start(), calls=%async_computation.20 | async-start | bytes 2621440 | tf_op jit(solution)/shard_map/all_gather | solution.py:173
  344.3 165.2 %copy-start.3 = (f32[256,1,1024]{2,0,1:T(8,128)}, f32[256,1,1024]{2,0,1:T(8,128)S(1)}, u32[]{:S(2)}) copy-start(f32[256,1,1024]{2,0,1:T(8,128)S(1)} %get-tuple-element.649) | copy-start | bytes 3145732
  345.7 163.8 %reduce-scatter.21.cloned.1.call-start = ((), (), s32[]{:S(2)}) async-start(), calls=%async_computation.21 | async-start | bytes 2621440 | tf_op jit(solution)/shard_map/reduce_scatter | solution.py:183
  466.8 72.6 %all-gather.47.cloned.1.call-start = ((), (), s32[]{:S(2)}) async-start(), calls=%async_computation.44 | async-start | bytes 2359296 | tf_op jit(solution)/shard_map/all_gather | solution.py:208
  467.5 119.9 %all-gather.29.cloned.1.call-start = ((), (), s32[]{:S(2)}) async-start(), calls=%async_computation.22 | async-start | bytes 2621440 | tf_op jit(solution)/shard_map/all_gather | solution.py:173
  512.2 121.5 %all-gather.31.cloned.1.call-start = ((), (), s32[]{:S(2)}) async-start(), calls=%async_computation.24 | async-start | bytes 2621440 | tf_op jit(solution)/shard_map/all_gather | solution.py:176
  514.4 148.2 %all-gather.49.cloned.1.call-start = ((), (), s32[]{:S(2)}) async-start(), calls=%async_computation.45 | async-start | bytes 2359296 | tf_op jit(solution)/shard_map/all_gather | solution.py:209
  515.0 203.9 %reduce-scatter.25.cloned.1.call-start = ((), (), s32[]{:S(2)}) async-start(), calls=%async_computation.25 | async-start | bytes 2621440 | tf_op jit(solution)/shard_map/reduce_scatter | solution.py:195
  674.9 89.4 %reduce-scatter.23.cloned.1.call-start = ((), (), s32[]{:S(2)}) async-start(), calls=%async_computation.23 | async-start | bytes 2621440 | tf_op jit(solution)/shard_map/reduce_scatter | solution.py:183
  680.8 83.5 %copy-start.92 = (f32[1,1,1024]{2,1,0:T(1,128)S(1)}, f32[1,1,1024]{2,1,0:T(1,128)}, u32[]{:S(2)}) copy-start(f32[1,1,1024]{2,1,0:T(1,128)} %get-tuple-element.772) | copy-start | bytes 12292
  680.8 132.8 %all-gather.33.cloned.1.call-start = ((), (), s32[]{:S(2)}) async-start(), calls=%async_computation.26 | async-start | bytes 2621440 | tf_op jit(solution)/shard_map/all_gather | solution.py:176
  768.3 152.5 %reduce-scatter.27.cloned.1.call-start = ((), (), s32[]{:S(2)}) async-start(), calls=%async_computation.27 | async-start | bytes 2621440 | tf_op jit(solution)/shard_map/reduce_scatter | solution.py:195
  878.0 93.2 %copy-start.101 = (f32[1,1024]{1,0:T(1,128)S(1)}, f32[1,1024]{1,0:T(1,128)}, u32[]{:S(2)}) copy-start(f32[1,1024]{1,0:T(1,128)} %copy-done.100) | copy-start | bytes 12292
  878.0 93.2 %all-gather.35.cloned.1.call-start = ((), (), s32[]{:S(2)}) async-start(), calls=%async_computation.28 | async-start | bytes 2621440 | tf_op jit(solution)/shard_map/all_gather | solution.py:176
  925.8 100.6 %reduce-scatter.29.cloned.1.call-start = ((), (), s32[]{:S(2)}) async-start(), calls=%async_computation.29 | async-start | bytes 2621440 | tf_op jit(solution)/shard_map/reduce_scatter | solution.py:195
  983.7 93.8 %all-gather.37.cloned.1.call-start = ((), (), s32[]{:S(2)}) async-start(), calls=%async_computation.30 | async-start | bytes 2621440 | tf_op jit(solution)/shard_map/all_gather | solution.py:176
  1032.0 129.2 %reduce-scatter.47.cloned.1.call-start = ((), (), s32[]{:S(2)}) async-start(), calls=%async_computation.39 | async-start | bytes 4718592 | tf_op jit(solution)/shard_map/reduce_scatter | solution.py:338
  1038.7 147.2 %reduce-scatter.45.cloned.1.call-start = ((), (), s32[]{:S(2)}) async-start(), calls=%async_computation.38 | async-start | bytes 4718592 | tf_op jit(solution)/shard_map/reduce_scatter | solution.py:338
  1046.4 194.5 %reduce-scatter.43.cloned.1.call-start = ((), (), s32[]{:S(2)}) async-start(), calls=%async_computation.37 | async-start | bytes 4718592 | tf_op jit(solution)/shard_map/reduce_scatter | solution.py:337
  1054.1 241.5 %reduce-scatter.41.cloned.1.call-start = ((), (), s32[]{:S(2)}) async-start(), calls=%async_computation.36 | async-start | bytes 4718592 | tf_op jit(solution)/shard_map/reduce_scatter | solution.py:337
  1061.6 273.4 %reduce-scatter.39.cloned.1.call-start = ((), (), s32[]{:S(2)}) async-start(), calls=%async_computation.35 | async-start | bytes 1179648 | tf_op jit(solution)/shard_map/reduce_scatter | solution.py:336
  1065.1 309.4 %reduce-scatter.37.cloned.1.call-start = ((), (), s32[]{:S(2)}) async-start(), calls=%async_computation.34 | async-start | bytes 1179648 | tf_op jit(solution)/shard_map/reduce_scatter | solution.py:336
  1084.5 336.2 %reduce-scatter.31.cloned.1.call-start = ((), (), s32[]{:S(2)}) async-start(), calls=%async_computation.31 | async-start | bytes 2621440 | tf_op jit(solution)/shard_map/reduce_scatter | solution.py:195
  1145.1 325.1 %reduce-scatter.35.cloned.1.call-start = ((), (), s32[]{:S(2)}) async-start(), calls=%async_computation.33 | async-start | bytes 3538944 | tf_op jit(solution)/shard_map/reduce_scatter | solution.py:335
  1150.7 369.3 %reduce-scatter.33.cloned.1.call-start = ((), (), s32[]{:S(2)}) async-start(), calls=%async_computation.32 | async-start | bytes 3538944 | tf_op jit(solution)/shard_map/reduce_scatter | solution.py:335
  1160.7 137.2 %copy-start.29 = (bf16[1024,1,4,64]{0,3,2,1:T(8,128)(2,1)S(1)}, bf16[1024,1,4,64]{0,3,2,1:T(8,128)(2,1)}, u32[]{:S(2)}) copy-start(bf16[1024,1,4,64]{0,3,2,1:T(8,128)(2,1)} %copy-done.28) | copy-start | bytes 1572868
  1186.0 234.8 %copy-start.2 = (bf16[256,1,1024]{2,0,1:T(8,128)(2,1)S(1)}, bf16[256,1,1024]{2,0,1:T(8,128)(2,1)}, u32[]{:S(2)}) copy-start(bf16[256,1,1024]{2,0,1:T(8,128)(2,1)} %param.29) | copy-start | bytes 1572868
  1186.0 234.8 %copy-start.63 = (f32[1,1,1024]{2,1,0:T(1,128)S(1)}, f32[1,1,1024]{2,1,0:T(1,128)}, u32[]{:S(2)}) copy-start(f32[1,1,1024]{2,1,0:T(1,128)} %copy-done.62) | copy-start | bytes 12292
  1186.0 234.8 %copy-start.72 = (f32[256]{0:T(256)S(1)}, f32[256]{0:T(256)}, u32[]{:S(2)}) copy-start(f32[256]{0:T(256)} %copy-done.71) | copy-start | bytes 3076
  1186.0 234.8 %copy-start.89 = (f32[256]{0:T(256)S(1)}, f32[256]{0:T(256)}, u32[]{:S(2)}) copy-start(f32[256]{0:T(256)} %copy-done.88) | copy-start | bytes 3076
  1188.3 234.1 %copy-start.33 = (f32[256,1,1024]{2,0,1:T(8,128)S(1)}, f32[256,1,1024]{2,0,1:T(8,128)}, u32[]{:S(2)}) copy-start(f32[256,1,1024]{2,0,1:T(8,128)} %get-tuple-element.637) | copy-start | bytes 3145732
  (95 other events, 2122.7 us)
Sparse Core Ops, SparseCore 0:
  10.5 29.1 all-gather.38
  41.8 45.9 all-gather.22
  143.1 42.5 reduce-scatter.16
  188.2 27.1 all-gather.40
  217.5 45.9 all-gather.24
  266.0 26.9 all-gather.42
  299.0 43.8 reduce-scatter.18
  345.4 25.1 all-gather.44
  372.8 45.9 all-gather.26
  466.9 42.5 reduce-scatter.20
  512.2 27.1 all-gather.46
  541.5 45.9 all-gather.28
  589.1 44.5 all-gather.30
  635.6 26.9 all-gather.48
  675.0 43.8 reduce-scatter.24
  721.0 43.1 reduce-scatter.22
  768.4 45.2 all-gather.32
  878.2 42.5 reduce-scatter.26
  926.0 45.2 all-gather.34
  983.8 42.5 reduce-scatter.28
  1032.1 45.2 all-gather.36
  1081.1 50.0 reduce-scatter.46
  1134.6 51.2 reduce-scatter.44
  1189.5 51.3 reduce-scatter.42
  1244.3 51.2 reduce-scatter.40
  1298.9 36.0 reduce-scatter.38
  1338.4 36.0 reduce-scatter.36
  1376.8 43.8 reduce-scatter.30
  1424.1 46.0 reduce-scatter.34
  1473.8 46.1 reduce-scatter.32
